TPU v7x, 32 devices: a whole 2x2x4 slice. The times are simulated.
32 devices in a mesh: rep: 8 (over z, x), fsdp: 4 (over y, core).
Axes of the slice: x: 2, y: 2, z: 4, core: 2. Of those that a mesh axis runs over, the one named last changes fastest.
Arguments:
- tokens: bfloat16 [32768, 768], P(('rep', 'fsdp')), may hold values from -6 to 6
- cotangent: bfloat16 [32768, 768], P(('rep', 'fsdp')), may hold values from -6 to 6
- lengths: int32 [32, 4], P(('rep', 'fsdp')), may hold values from 0 to 1024, as said below
- w_qkv: float32 [768, 2304], P('fsdp'), may hold values from -0.21875 to 0.21875
- m_qkv: float32 [768, 2304], P('fsdp'), may hold values from -192 to 192
- v_qkv: float32 [768, 2304], P('fsdp'), may hold values from 4915.2 to 19660.8
- w_proj: float32 [768, 768], P('fsdp'), may hold values from -2 to 2
- m_proj: float32 [768, 768], P('fsdp'), may hold values from -20 to 20
- v_proj: float32 [768, 768], P('fsdp'), may hold values from 48 to 192
- w_ffn: float32 [768, 4096], P('fsdp'), may hold values from -0.21875 to 0.21875
- m_ffn: float32 [768, 4096], P('fsdp'), may hold values from -112 to 112
- v_ffn: float32 [768, 4096], P('fsdp'), may hold values from 1507.328 to 5898.24
- w_down: float32 [2048, 768], P('fsdp'), may hold values from -0.25 to 0.25
- m_down: float32 [2048, 768], P('fsdp'), may hold values from -56 to 56
- v_down: float32 [2048, 768], P('fsdp'), may hold values from 360.448 to 1507.328
- gains: float32 [2, 768], P(None, 'fsdp'), may hold values from 0.5 to 1.5
- m_gains: float32 [2, 768], P(None, 'fsdp'), may hold values from -320 to 320
- v_gains: float32 [2, 768], P(None, 'fsdp'), may hold values from 11468.8 to 45875.2
Outputs:
- block_out: bfloat16 [32768, 768], P(('rep', 'fsdp'))
- input_grad: float32 [32768, 768], P(('rep', 'fsdp'))
- qkv_moment: float32 [768, 2304], P('fsdp')
- qkv_second: float32 [768, 2304], P('fsdp')
- qkv_weight: float32 [768, 2304], P('fsdp')
- proj_moment: float32 [768, 768], P('fsdp')
- proj_second: float32 [768, 768], P('fsdp')
- proj_weight: float32 [768, 768], P('fsdp')
- ffn_moment: float32 [768, 4096], P('fsdp')
- ffn_second: float32 [768, 4096], P('fsdp')
- ffn_weight: float32 [768, 4096], P('fsdp')
- down_moment: float32 [2048, 768], P('fsdp')
- down_second: float32 [2048, 768], P('fsdp')
- down_weight: float32 [2048, 768], P('fsdp')
- gain_moment: float32 [2, 768], P(None, 'fsdp')
- gain_second: float32 [2, 768], P(None, 'fsdp')
- gain_weight: float32 [2, 768], P(None, 'fsdp')
Inputs may be any that keep to these rules, and one draw needn't show every extreme that they name: A buffer's sequences lie end to end from its first row, and its lengths sum to at most 1024; rows after them are padding. Zero lengths may occur. In every draw one buffer holds a single sequence of 1024 tokens.
All inputs are finite; a program needn't handle non-finite values.
Results may differ from a plain program's by a relative error of at most 0.022.
Values may be sent and summed in bfloat16 or wider, within the bound.
A program may use at most 320 MiB of HBM per device.

v0:
```python
import functools

import jax
import jax.numpy as jnp
import numpy as np
from jax import lax
from jax.experimental import pallas as pl
from jax.experimental.pallas import tpu as pltpu
from jax.sharding import PartitionSpec as P

HEADS = 12
FF = 2048
STEP = 10
norm_eps = 1e-05
rope_base = 10000.0
beta_first = 0.9
beta_second = 0.95
adam_eps = 1e-08
decay_rate = 0.1
LOG2E = 1.4426950408889634
MASKED = -1e30
MESH = pl.DeviceIdType.MESH
f32 = jnp.float32
bf16 = jnp.bfloat16
BLK = 256
CHUNKS = 12
PIECE = 144
SLOTS = 9
LAGS = (2, 2, 2, 2, 2)
ANY = pl.BlockSpec(memory_space=pl.ANY)
VM = pl.BlockSpec(memory_space=pltpu.VMEM)
SM = pl.BlockSpec(memory_space=pltpu.SMEM)


def dot(a, b, ca, cb):
    return lax.dot_general(a, b, (((ca,), (cb,)), ((), ())), preferred_element_type=f32)


def joined(ref, first, number):
    return jnp.concatenate([ref[first + i] for i in range(number)], axis=1)


def rows_of(i):
    return pl.ds(pl.multiple_of(i * BLK, BLK), BLK)


def lane_head(h, shape):
    return (lax.broadcasted_iota(jnp.int32, shape, 1) // 64) == h


def seq_ends(len_ref):
    total = 0
    ends = []
    for j in range(4):
        total = total + len_ref[0, j]
        ends.append(total)
    return ends


def fill_bias(ends, bias, count):
    q = lax.broadcasted_iota(jnp.int32, (1, count), 1)
    sq = sum((q >= e).astype(jnp.int32) for e in ends)

    @pl.loop(0, count // BLK)
    def _(j):
        k = lax.broadcasted_iota(jnp.int32, (BLK, 1), 0) + j * BLK
        sk = sum((k >= e).astype(jnp.int32) for e in ends)
        bias[rows_of(j), :] = jnp.where((sk == sq) & (k <= q), 0.0, MASKED)


def rope(block, cosine, sine, sign):
    lane = lax.broadcasted_iota(jnp.int32, block.shape, 1)
    swapped = jnp.where(lane % 64 < 32, pltpu.roll(block, 96, 1), pltpu.roll(block, 32, 1))
    if sign > 0:
        return block * cosine + swapped * sine
    return block * cosine - swapped * sine


def remote(src, dst, send_sem, recv_sem, device):
    return pltpu.make_async_remote_copy(
        src_ref=src, dst_ref=dst, send_sem=send_sem, recv_sem=recv_sem,
        device_id=device, device_id_type=MESH)


def unit_rows(value):
    inverse = lax.rsqrt(jnp.mean(value * value, axis=-1, keepdims=True) + norm_eps)
    return value * inverse, inverse


class Gather:
    def __init__(self, own, full, first, blocks, shard_rows, sems, index, ids, direct=False):
        self.direct = direct
        self.own, self.full, self.first, self.blocks, self.n = own, full, first, blocks, shard_rows
        self.ssem, self.rsem, self.w, self.ids = sems[0], sems[1], index, ids
        rep, fs = ids["rep"], ids["fsdp"]
        self.b0, self.b1 = rep % 2, (rep // 2) % 2
        self.q = rep % 4
        self.far = (fs + 2) % 4
        self.fs = fs
        self.quarter = shard_rows // 4

    def part(self, shard, quarter, quarters, half=None):
        row = pl.multiple_of(shard * self.n + quarter * self.quarter, 16)
        first, blocks = self.first, self.blocks
        if half is not None:
            blocks = blocks // 2
            first = first + half * blocks
        return self.full.at[pl.ds(first, blocks), pl.ds(row, quarters * self.quarter), :]

    def cp(self, i, ref, device, src=None):
        return remote(ref if src is None else src, ref, self.ssem.at[self.w, i], self.rsem.at[self.w, i], device)

    def copy(self, i):
        d = self.ids
        p, far, fs, q = self.part, self.far, self.fs, self.q
        q1 = (1 - self.b0) + 2 * self.b1
        q2 = self.b0 + 2 * (1 - self.b1)
        q3 = (1 - self.b0) + 2 * (1 - self.b1)
        own = own_quarter = None
        if self.own is not None:
            own = self.own.at[pl.ds(self.first, self.blocks)]
            own_quarter = self.own.at[pl.ds(self.first, self.blocks), pl.ds(pl.multiple_of(q * self.quarter, 16), self.quarter), :]
        if self.direct and i:
            return self.cp(i, p(fs if i == 1 else far, 0, 4), d["y" if i == 1 else "core"])
        return [
            lambda: self.cp(0, p(fs, 0, 4), d["core"], own),
            lambda: self.cp(1, p(fs, q, 1), d["y"], own_quarter),
            lambda: self.cp(2, p(far, q, 1, 0), d["bit0"]),
            lambda: self.cp(3, p(far, q, 1, 1), d["bit1"]),
            lambda: self.cp(4, p(far, q, 1), d["core"]),
            lambda: self.cp(5, p(far, 2 * self.b1, 2, 0), d["bit1"]),
            lambda: self.cp(6, p(far, q, 1, 1), d["bit0"]),
            lambda: self.cp(7, p(far, q2, 1, 1), d["bit0"]),
            lambda: self.cp(8, p(far, q1, 1, 0), d["core"]),
            lambda: self.cp(9, p(far, q2, 1, 1), d["core"]),
            lambda: self.cp(10, p(far, 2 * (1 - self.b1), 2, 0), d["core"]),
            lambda: self.cp(11, p(far, q1, 1, 1), d["core"]),
            lambda: self.cp(12, p(far, q3, 1, 1), d["core"]),
        ][i]()

    def step(self, waits, starts):
        for i in waits:
            self.copy(i).wait_recv()
        for i in starts:
            self.copy(i).start()

    def start(self):
        self.step((), (1, 0))

    def second(self):
        self.step((1,), (4,) if self.direct else (2, 3, 4))

    def third(self):
        self.step((2, 3), (5, 6, 7, 8, 9))

    def fourth(self):
        self.step((5, 6, 7), (10, 11, 12))

    def arrive(self):
        self.step((0, 4) if self.direct else (0, 4, 8, 9, 10, 11, 12), ())

    def sent(self):
        for i in (0, 1, 4) if self.direct else range(13):
            self.copy(i).wait_send()


def partners(rep, fs, reps):
    found = {"rep": rep, "fsdp": fs, "core": (rep, fs ^ 1), "y": (rep, fs ^ 2)}
    for b in range(reps.bit_length() - 1):
        found["bit%d" % b] = (rep ^ (1 << b), fs)
    for d in (1, 2, 3):
        found["z%d" % d] = (rep ^ (2 * (d // 2) + 4 * (d % 2)), fs)
    return found


def meet(ids, names):
    barrier = pltpu.get_barrier_semaphore()
    for name in names:
        pl.semaphore_signal(barrier, inc=1, device_id=ids[name], device_id_type=MESH)
    pl.semaphore_wait(barrier, len(names))


def place_gains(ref, rows, fs):
    ref[...] = pltpu.roll(ref[...], fs * rows, 1)


def forward_kernel(reps, len_ref, x_in, gain_in, freq_ref, wq_in, wo_in, wf_in, wd_in,
                   wq_out, wo_out, wf_out, wd_out, q_out, k_out, v_out, a_out, at_out, h1t_out, log_out, mid_out, gain_out, cos_out, sin_out,
                   wq_s, wo_s, st_q, st_o, st_f, st_d, own_f, own_d, gain_a, gain_b, gain_c, x_s, cos_s, sin_s,
                   h1_s, h1t_s, q_s, k_s, vt_s, v_s, a_s, at_s, log_s, mid_s, bias,
                   load_sem, store_sem, send_sem, recv_sem, gsend_sem, grecv_sem):
    count, width = x_s.shape
    pairs = width // 128
    rows = width // 4
    rep, fs = lax.axis_index("rep"), lax.axis_index("fsdp")
    ids = partners(rep, fs, reps)
    load_q = pltpu.make_async_copy(wq_in, st_q, load_sem.at[0])
    load_x = pltpu.make_async_copy(x_in, x_s, load_sem.at[1])
    load_o = pltpu.make_async_copy(wo_in, st_o, load_sem.at[2])
    load_f = pltpu.make_async_copy(wf_in, st_f, load_sem.at[3])
    load_d = pltpu.make_async_copy(wd_in, st_d, load_sem.at[4])
    for c in (load_q, load_x, load_o, load_f, load_d):
        c.start()
    gain_a[...] = jnp.zeros_like(gain_a)
    gain_a[0:2, 0:rows] = gain_in[...].astype(bf16).astype(f32)
    gain_a[...] = pltpu.roll(gain_a[...], fs * rows, 1)
    meet(ids, ("core", "y", "bit0", "bit1"))

    sems = (send_sem, recv_sem)
    near = [Gather(None, wq_s, 6 * c, 6, rows, sems, c, ids, c == 0) for c in range(3)]
    proj = Gather(None, wo_s, 0, 6, rows, sems, 3, ids)
    wide = [Gather(own_f, wf_out, 8 * j, 8, rows, sems, 4 + j, ids) for j in range(4)]
    down = Gather(own_d, wd_out, 0, 4, FF // 16, sems, 8, ids)

    g_core = remote(gain_a, gain_b, gsend_sem.at[0], grecv_sem.at[0], ids["core"])
    g_core.start()
    own_rows = pl.ds(pl.multiple_of(fs * rows, 16), rows)
    load_q.wait()
    for c in range(3):
        for t in range(3):
            for i in range(2):
                col = t * width + (2 * c + i) * 128
                wq_s[6 * c + 2 * t + i, own_rows, :] = st_q[:, col:col + 128].astype(bf16)
        if c < 2:
            near[c].start()
    load_o.wait()
    load_f.wait()
    for j in range(4):
        for n in range(8):
            col = (4 * n + j) * 128
            own_f[8 * j + n] = st_f[:, col:col + 128].astype(bf16)
    for i in range(6):
        wo_s[i, own_rows, :] = st_o[:, 128 * i:128 * i + 128].astype(bf16)
    load_d.wait()
    for j in range(4):
        own_d[j] = st_d[128 * j:128 * j + 128, :].astype(bf16)
    g_core.wait()
    gain_c[0] = gain_a[...] + gain_b[...]
    g_y = remote(gain_c.at[0], gain_c.at[1], gsend_sem.at[1], grecv_sem.at[1], ids["y"])
    g_y.start()
    near[1].second()
    near[2].start()
    wide[0].start()
    stores = [
        pltpu.make_async_copy(own_f, wf_out.at[:, own_rows, :], store_sem.at[0]),
        pltpu.make_async_copy(own_d, wd_out.at[:, pl.ds(pl.multiple_of(fs * (FF // 16), 16), FF // 16), :], store_sem.at[1]),
    ]
    for c in stores:
        c.start()
    ends = seq_ends(len_ref)
    token = lax.broadcasted_iota(jnp.int32, (1, count), 1)
    start = jnp.zeros((1, count), jnp.int32)
    for e in ends:
        start = jnp.where(token >= e, e, start)
    angle = freq_ref[:, 0:1] * (token - start).astype(f32)
    cosine, sine = jnp.cos(angle), jnp.sin(angle)
    cos_s[...] = jnp.concatenate([cosine] * 4, axis=0).T
    sin_s[...] = jnp.concatenate([-sine, sine, -sine, sine], axis=0).T
    near[2].second()
    wide[1].start()
    proj.start()
    near[1].third()
    g_y.wait()
    gain_out[...] = gain_c[0] + gain_c[1]
    g1 = gain_out[0:1, :]
    load_x.wait()

    @pl.loop(0, count // BLK)
    def _(i):
        blk = pl.ds(pl.multiple_of(i * BLK, BLK), BLK)
        x = x_s[blk, :].astype(f32)
        inverse = lax.rsqrt(jnp.mean(x * x, axis=-1, keepdims=True) + norm_eps)
        h1 = x * inverse * g1
        h1_s[blk, :] = h1.astype(bf16)
        h1t_s[:, blk] = h1.T.astype(bf16)

    near[0].second()
    wide[0].second()
    wide[2].start()
    near[2].third()
    fill_bias(ends, bias, count)
    near[1].fourth()
    wide[3].start()

    def project(c):
        h1 = h1_s[...]
        for t in range(3):
            block = dot(h1, joined(wq_s, 6 * c + 2 * t, 2), 1, 0)
            for i in range(2):
                p = 2 * c + i
                piece = block[:, 128 * i:128 * i + 128]
                if t == 0:
                    q_s[p] = (rope(piece, cos_s[...], sin_s[...], 1) * (LOG2E / 8)).astype(bf16)
                elif t == 1:
                    k_s[p] = rope(piece, cos_s[...], sin_s[...], 1).astype(bf16)
                else:
                    v_s[p] = piece.astype(bf16)
                    vt_s[p] = piece.T.astype(bf16)

    def scores(p, i, h):
        q = q_s[p, i * BLK:(i + 1) * BLK, :]
        return dot(k_s[p, :BLK * (i + 1), :], jnp.where(lane_head(h, q.shape), q, 0), 1, 1)

    def soft(p, i, h, s):
        s = s + bias[:BLK * (i + 1), i * BLK:(i + 1) * BLK]
        largest = jnp.max(s, axis=0, keepdims=True)
        e = jnp.exp2(s - largest)
        total = jnp.sum(e, axis=0, keepdims=True)
        log_s[p, h:h + 1, i * BLK:(i + 1) * BLK] = largest + jnp.log2(total)
        return e.astype(bf16), total

    def mix(p, i, h, e, total):
        return dot(vt_s[p, 64 * h:64 * h + 64, :BLK * (i + 1)], e, 1, 0) * (1.0 / total)

    def attend(p):
        tasks = [(i, h) for i in range(count // BLK) for h in range(2)]
        s = scores(p, *tasks[0])
        held = None
        outs = {}
        for n, task in enumerate(tasks):
            ahead = scores(p, *tasks[n + 1]) if n + 1 < len(tasks) else None
            weighted = soft(p, *task, s)
            if held is not None:
                outs[held[0]] = mix(p, *held[0], *held[1])
            held = (task, weighted)
            s = ahead
        outs[held[0]] = mix(p, *held[0], *held[1])
        cols = pl.ds(pl.multiple_of(p * 128, 128), 128)
        for i in range(count // BLK):
            both = jnp.concatenate([outs[i, 0], outs[i, 1]], axis=0)
            at_s[cols, i * BLK:(i + 1) * BLK] = both.astype(bf16)
            a_s[i * BLK:(i + 1) * BLK, cols] = both.T.astype(bf16)

    ready = [pltpu.make_async_copy(src, dst, store_sem.at[3 + i]) for i, (src, dst) in enumerate((
        (wq_s, wq_out), (q_s, q_out), (k_s, k_out), (v_s, v_out), (cos_s, cos_out), (sin_s, sin_out), (h1t_s, h1t_out)))]
    arrivals = [[near[0].arrive], [near[1].arrive], [near[2].arrive]]
    projected = [
        [near[2].fourth, wide[1].second, wide[0].third, down.start],
        [down.second, proj.third],
        [c.start for c in ready],
    ]
    attended = [
        [wide[1].third, wide[2].second, proj.second],
        [wide[0].fourth, wide[3].second, wide[2].third],
        [wide[1].fourth, wide[3].third],
        [wide[2].fourth, down.third, proj.fourth],
        [wide[3].fourth],
        [down.fourth],
    ]

    def at_turn(c, lists):
        for turn, steps in enumerate(lists):
            if steps:
                @pl.when(c == turn)
                def _():
                    for step in steps:
                        step()

    @pl.loop(0, 3)
    def _(c):
        at_turn(c, arrivals)
        project(c)
        at_turn(c, projected)

        @pl.loop(2 * c, 2 * c + 2)
        def _(p):
            attend(p)
            at_turn(p, attended)
    stores += ready
    proj.arrive()
    for i, (src, dst) in enumerate(((wo_s, wo_out), (a_s, a_out), (at_s, at_out), (log_s, log_out))):
        c = pltpu.make_async_copy(src, dst, store_sem.at[10 + i])
        c.start()
        stores.append(c)

    @pl.loop(0, count // BLK)
    def _(i):
        blk = pl.ds(pl.multiple_of(i * BLK, BLK), BLK)
        mid_s[blk, :] = x_s[blk, :].astype(f32) + dot(a_s[blk, :], joined(wo_s, 0, 6), 1, 0)
    c = pltpu.make_async_copy(mid_s, mid_out, store_sem.at[14])
    c.start()
    stores.append(c)
    for g in wide + [down]:
        g.arrive()
    for g in near + [proj] + wide + [down]:
        g.sent()
    for c in stores:
        c.wait()


def frequencies():
    half = 32
    frequency = rope_base ** (-2.0 * np.arange(half) / (2 * half))
    return jnp.asarray(np.broadcast_to(frequency[:, None], (half, 128)), f32)


def forward(reps, lengths, tokens, gains, w_qkv, w_proj, w_ffn, w_down):
    count, width = tokens.shape
    pairs = width // 128
    S = jax.ShapeDtypeStruct
    V = pltpu.VMEM
    rows = width // 4
    dma = pltpu.SemaphoreType.DMA
    return pl.pallas_call(
        functools.partial(forward_kernel, reps),
        name="gather_forward",
        in_specs=[SM, ANY, VM, VM, ANY, ANY, ANY, ANY],
        out_specs=[ANY] * 12 + [VM] + [ANY] * 2,
        out_shape=[S((18, width, 128), bf16), S((6, width, 128), bf16), S((32, width, 128), bf16), S((4, FF // 4, width), bf16),
                   S((pairs, count, 128), bf16), S((pairs, count, 128), bf16), S((pairs, count, 128), bf16),
                   S((count, width), bf16), S((width, count), bf16), S((width, count), bf16), S((pairs, 8, count), f32),
                   S((count, width), f32), S((8, width), f32),
                   S((count, 128), f32), S((count, 128), f32)],
        scratch_shapes=[
            V((18, width, 128), bf16), V((6, width, 128), bf16), V((rows, 3 * width), f32), V((rows, width), f32),
            V((rows, 2 * FF), f32), V((FF // 4, width), f32), V((32, rows, 128), bf16), V((4, FF // 16, width), bf16),
            V((8, width), f32), V((8, width), f32), V((2, 8, width), f32),
            V((count, width), bf16), V((count, 128), f32), V((count, 128), f32),
            V((count, width), bf16), V((width, count), bf16), V((pairs, count, 128), bf16), V((pairs, count, 128), bf16),
            V((pairs, 128, count), bf16), V((pairs, count, 128), bf16), V((count, width), bf16), V((width, count), bf16),
            V((pairs, 8, count), f32), V((count, width), f32), V((count, count), f32),
            dma((5,)), dma((15,)), dma((9, 13)), dma((9, 13)), dma((2,)), dma((2,))],
        compiler_params=pltpu.CompilerParams(collective_id=0, has_side_effects=True, vmem_limit_bytes=60 * 2**20),
    )(lengths, tokens, gains, frequencies(), w_qkv, w_proj, w_ffn, w_down)


class Reduce:
    def __init__(self, ids, reps, grad, slots, kept, out, sems, out_sem):
        self.ids = ids
        self.grad, self.slots, self.kept, self.out = grad, slots, kept, out
        self.ssem, self.rsem = sems
        self.out_sem = out_sem
        rep, fs = ids["rep"], ids["fsdp"]
        self.core, self.y = fs % 2, fs // 2
        self.half = rep % 2
        self.z = 2 * (rep // 2 % 2) + rep // 4 % 2
        self.extra = reps.bit_length() - 1 - 3
        self.stages = 7 + self.extra
        self.offsets = stage_offsets(reps)
        self.lags = stage_lags(reps)

    def cp(self, kind, par, src, dst, device):
        return remote(src, dst, self.ssem.at[kind, par], self.rsem.at[kind, par], self.ids[device])

    def exchange(self, k, n):
        g = self.grad.at[n % SLOTS]
        mine = g.at[self.core, self.y]
        keep = self.kept.at[n]
        par = n % (2 * self.lags[k])
        first = 4 * self.half
        own = keep.at[pl.ds(first + self.z, 1)]
        if k == 0:
            return [self.cp(0, par, g.at[1 - self.core], self.slots[0].at[par], "core")]
        if k == 1:
            return [self.cp(1, par, g.at[self.core, 1 - self.y], self.slots[1].at[par], "y")]
        if k == 2:
            return [self.cp(2, par, mine.at[pl.ds(4 - first, 4)], self.slots[2].at[par], "bit0")]
        if k == 3:
            return [self.cp(2 + d, par, mine.at[first + (self.z ^ d)], self.slots[3].at[par, d - 1], "z%d" % d) for d in (1, 2, 3)]
        if k < 4 + self.extra:
            return [self.cp(6 + k, par, own, self.slots[k].at[par], "bit%d" % (k - 1))]
        if k == 4 + self.extra:
            return [self.cp(5 + d, par, own, own, "z%d" % d) for d in (1, 2, 3)]
        part = keep.at[pl.ds(first, 4)]
        return [self.cp(9, par, part, part, "bit0")]

    def start(self, k, n):
        for c in self.exchange(k, n):
            c.start()

    def add(self, n, first, number, slot, offset):
        mine = self.grad.at[n % SLOTS, self.core, self.y]

        @pl.loop(0, number)
        def _(i):
            mine[first + i] = (mine[first + i].astype(f32) + slot[offset + i].astype(f32)).astype(bf16)

    def stage(self, k, n):
        par = n % (2 * self.lags[k - 1])
        first = 4 * self.half
        if k > 0:
            for c in self.exchange(k - 1, n):
                c.wait()
        if k == 0:
            self.start(0, n)
        elif k == 1:
            g, slot = self.grad.at[n % SLOTS, self.core], self.slots[0].at[par]
            for y in (1 - self.y, self.y):
                @pl.loop(0, 8)
                def _(i):
                    g[y, i] = (g[y, i].astype(f32) + slot[y, i].astype(f32)).astype(bf16)
                if y is not self.y:
                    self.start(1, n)
        elif k == 2:
            self.add(n, 4 - first, 4, self.slots[1].at[par], 4 - first)
            self.start(2, n)
            self.add(n, first, 4, self.slots[1].at[par], first)
        elif k == 3:
            self.add(n, first, 4, self.slots[2].at[par], 0)
            self.start(3, n)
        elif k == 4:
            own = first + self.z
            slot = self.slots[3].at[par]
            total = self.grad[n % SLOTS, self.core, self.y, own].astype(f32) + slot[0].astype(f32)
            self.kept[n, own] = (total + slot[1].astype(f32) + slot[2].astype(f32)).astype(bf16)
            self.start(4, n)
        elif k <= 4 + self.extra:
            own = first + self.z
            slot = self.slots[k - 1].at[par]
            self.kept[n, own] = (self.kept[n, own].astype(f32) + slot[0].astype(f32)).astype(bf16)
            self.start(k, n)
        elif k < self.stages - 1:
            self.start(k, n)
        else:
            self.store(n).start()

    def store(self, n):
        return pltpu.make_async_copy(self.kept.at[n], self.out.at[n], self.out_sem.at[n])

    def tick(self, time):
        for k in reversed(range(self.stages)):
            since = time - self.offsets[k]
            if isinstance(time, int):
                if since < 0 or (since > 8 and since % 2) or since > 2 * CHUNKS - 10:
                    continue
                self.stage(k, since if since <= 8 else (since + 8) // 2)
            else:
                late = (since + 8) // 2
                fits = jnp.logical_and(since >= 0, jnp.logical_or(since <= 8, jnp.logical_and(since == 2 * late - 8, late < CHUNKS)))

                @pl.when(fits)
                def _():
                    self.stage(k, jnp.where(since <= 8, since, late))

    def last_tick(self):
        return 2 * CHUNKS - 10 + self.offsets[-1]


def stage_offsets(reps):
    stages = 7 + reps.bit_length() - 1 - 3
    return [0] + [1 + sum(LAGS[i] if i < len(LAGS) else LAGS[-1] for i in range(k)) for k in range(stages - 1)]


def stage_lags(reps):
    offsets = stage_offsets(reps)
    return [b - a for a, b in zip(offsets, offsets[1:])]


def put_pieces(slot, value, block):
    for s in range(4):
        for i in range(2):
            half, c = divmod(block + i, 3)
            for r in range(4):
                row = 192 * s + 48 * r
                slot[s % 2, s // 2, r + 4 * half, 48 * c:48 * c + 48, :] = value[row:row + 48, 128 * i:128 * i + 128]


def backward_kernel(reps, len_ref, gain_ref, x_in, cot_in, mid_in, q_in, k_in, v_in, a_in, at_in, h1t_in, log_in, cos_in, sin_in,
                    wq_in, wo_in, wf_in, wd_in,
                    block_out, input_grad, grad_out, gain_out,
                    mid_s, dmid_s, dy_s, x_s, cos_s, sin_s, wq_s, wo_s, out_s,
                    grad_s, kept_s, gain_s, send_sem, recv_sem, gsend_sem, grecv_sem, out_sem, load_sem, store_sem, *slots):
    count, width = x_s.shape
    rows = width // 4
    blocks = count // BLK
    rep, fs = lax.axis_index("rep"), lax.axis_index("fsdp")
    ids = partners(rep, fs, reps)
    bits = reps.bit_length() - 1
    names = ("core", "y") + tuple("bit%d" % b for b in range(bits))
    friends = names[:3] + ("z1", "z2", "z3") + names[5:]
    red = Reduce(ids, reps, grad_s, slots, kept_s, grad_out, (send_sem, recv_sem), out_sem)
    ends = seq_ends(len_ref)
    valid = ends[3]

    def load(i, src, dst):
        c = pltpu.make_async_copy(src, dst, load_sem.at[i])
        c.start()
        return c

    g1, g2 = gain_ref[0:1, :], gain_ref[1:2, :]

    def feed(wf_s, wd_s, h2_s, h2t_s, z_s, df_s):
        need = [load(0, mid_in, mid_s), load(1, cot_in, dy_s)]
        def weights(j):
            return [pltpu.make_async_copy(wf_in.at[pl.ds(8 * j, 8)], wf_s.at[pl.ds(8 * j, 8)], load_sem.at[2 + 2 * j]),
                    pltpu.make_async_copy(wd_in.at[j], wd_s.at[j], load_sem.at[3 + 2 * j])]

        for j in range(4):
            for c in weights(j):
                c.start()
        late = [load(10, x_in, x_s), load(11, cos_in, cos_s), load(12, sin_in, sin_s), load(13, wq_in, wq_s),
                load(14, wo_in, wo_s)]
        meet(ids, friends)
        for c in need:
            c.wait()

        @pl.loop(0, blocks)
        def _(i):
            blk = rows_of(i)
            unit, _ = unit_rows(mid_s[blk, :])
            h2 = unit * g2
            h2_s[blk, :] = h2.astype(bf16)
            h2t_s[:, blk] = h2.T.astype(bf16)
            token = lax.broadcasted_iota(jnp.int32, (BLK, 1), 0) + i * BLK
            dy_s[blk, :] = jnp.where(token < valid, dy_s[blk, :], 0)
            out_s[blk, :] = mid_s[blk, :]
            dmid_s[blk, :] = jnp.zeros((BLK, width), f32)

        @pl.loop(0, 4)
        def _(j):
            for c in weights(j):
                c.wait()

            @pl.loop(0, blocks)
            def _(i):
                blk = rows_of(i)
                h2 = h2_s[blk, :]
                gate = dot(h2, joined(wf_s, 8 * j, 4), 1, 0)
                up = dot(h2, joined(wf_s, 8 * j + 4, 4), 1, 0)
                dz = dot(dy_s[blk, :], wd_s[j], 1, 1)
                sg = 1.0 / (1.0 + jnp.exp(-gate))
                silu = gate * sg
                z = (silu * up).astype(bf16)
                z_s[blk, :] = z
                dgate = (dz * up * (sg * (1.0 + gate * (1.0 - sg)))).astype(bf16)
                dup = (dz * silu).astype(bf16)
                df_s[blk, 0:512] = dgate
                df_s[blk, 512:1024] = dup
                out_s[blk, :] += dot(z, wd_s[j], 1, 0)
                dmid_s[blk, :] += dot(jnp.concatenate([dgate, dup], axis=1), joined(wf_s, 8 * j, 8), 1, 1)

            red.tick(2 * j - 1)
            gwd = dot(z_s[...], dy_s[...], 0, 0).astype(bf16)
            for s in range(4):
                for k in range(8):
                    for c in range(6):
                        row = 128 * s + 16 * k
                        grad_s[2 * j, s % 2, s // 2, k, 16 * c:16 * c + 16, :] = gwd[row:row + 16, 128 * c:128 * c + 128]

            @pl.loop(0, 4)
            def _(n):
                gwf = dot(h2t_s[...], df_s[:, pl.ds(pl.multiple_of(256 * n, 256), 256)], 1, 0).astype(bf16)
                for s in range(4):
                    for i in range(2):
                        lanes = slice(128 * i, 128 * i + 128)
                        grad_s[2 * j, s % 2, s // 2, 2 * n + i, 96:144, :] = gwf[rows * s:rows * s + 48, lanes]
                        grad_s[2 * j + 1, s % 2, s // 2, 2 * n + i, 0:144, :] = gwf[rows * s + 48:rows * s + rows, lanes]
            red.tick(2 * j)
        for c in late:
            c.wait()

    V = pltpu.VMEM
    pl.run_scoped(feed, V((32, width, 128), bf16), V((4, FF // 4, width), bf16), V((count, width), bf16),
                  V((width, count), bf16), V((count, 512), bf16), V((count, 1024), bf16))

    def attention(q_s, k_s, v_s, kt_s, a_s, at_s, da_s, log_s, dmb_s, dq3_s, h1t_s, bias, dqt_s):
        need = [load(0, q_in, q_s), load(1, k_in, k_s), load(2, v_in, v_s), load(3, log_in, log_s), load(4, a_in, a_s),
                load(5, at_in, at_s), load(6, h1t_in, h1t_s)]

        gain_s[...] = jnp.zeros_like(gain_s)
        @pl.loop(0, blocks)
        def _(i):
            blk = rows_of(i)
            unit, inverse = unit_rows(mid_s[blk, :])
            dh = dmid_s[blk, :]
            gain_s[0, 1:2, :] += jnp.sum(dh * unit, axis=0, keepdims=True)
            scaled = dh * g2
            dmid = dy_s[blk, :].astype(f32) + inverse * (scaled - unit * jnp.mean(scaled * unit, axis=-1, keepdims=True))
            dmid_s[blk, :] = dmid
            dmb_s[blk, :] = dmid.astype(bf16)
            mid_s[blk, :] = out_s[blk, :]
        red.tick(7)
        for c in need:
            c.wait()

        @pl.loop(0, 3)
        def _(c):
            part = pl.ds(pl.multiple_of(c * 256, 256), 256)
            weight = jnp.concatenate([wo_s[i, part, :] for i in range(6)], axis=1)
            da = dot(dmb_s[...], weight, 1, 1).astype(bf16)
            da_s[2 * c] = da[:, 0:128]
            da_s[2 * c + 1] = da[:, 128:256]
        for n in range(3):
            gwo = dot(at_s[...], dmb_s[:, 256 * n:256 * n + 256], 1, 0).astype(bf16)
            put_pieces(grad_s.at[8], gwo, 2 * n)
        red.tick(8)
        fill_bias(ends, bias, count)

        def pair(p, place):
            kt_s[...] = k_s[p].T
            cols = pl.ds(pl.multiple_of(p * 128, 128), 128)
            product = da_s[p].astype(f32) * a_s[:, cols].astype(f32)
            pick = ((lax.broadcasted_iota(jnp.int32, (8, 128), 1) // 64)
                    == lax.broadcasted_iota(jnp.int32, (8, 128), 0)).astype(bf16)
            high = product.astype(bf16)
            low = (product - high.astype(f32)).astype(bf16)
            centred = dot(pick, high, 1, 1) + dot(pick, low, 1, 1)

            def first(j, h):
                lo = j * BLK
                q, da = q_s[p, lo:, :], da_s[p, lo:, :]
                mine = lane_head(h, q.shape)
                q, da = jnp.where(mine, q, 0), jnp.where(mine, da, 0)
                return dot(k_s[p, lo:lo + BLK, :], q, 1, 1), dot(v_s[p, lo:lo + BLK, :], da, 1, 1), q, da

            def middle(j, h, s, dp):
                lo = j * BLK
                weight = jnp.exp2(s + bias[lo:lo + BLK, lo:] - log_s[p, h:h + 1, lo:])
                ds = (weight * (dp - centred[h:h + 1, lo:])).astype(bf16)
                return weight.astype(bf16), ds

            sums = {}

            def last(j, h, weight, ds, q, da):
                lo = j * BLK
                dv, dk = dot(weight, da, 1, 0), dot(ds, q, 1, 0)
                dq = dot(kt_s[64 * h:64 * h + 64, lo:lo + BLK], ds, 1, 0)
                if j == 0:
                    dqt_s[64 * h:64 * h + 64, :] = dq
                else:
                    dqt_s[64 * h:64 * h + 64, lo:] += dq
                if j in sums:
                    dk, dv = dk + sums[j][0], dv + sums[j][1]
                    dk = rope(dk * (1.0 / LOG2E), cos_s[lo:lo + BLK, :], sin_s[lo:lo + BLK, :], -1)
                    dq3_s[place + 2, lo:lo + BLK, :] = dk.astype(bf16)
                    dq3_s[place + 4, lo:lo + BLK, :] = dv.astype(bf16)
                else:
                    sums[j] = (dk, dv)

            tasks = [(j, h) for j in range(blocks) for h in range(2)]
            now = first(*tasks[0])
            held = None
            for n, task in enumerate(tasks):
                ahead = first(*tasks[n + 1]) if n + 1 < len(tasks) else None
                pd = middle(*task, now[0], now[1])
                if held is not None:
                    last(*held)
                held = (*task, *pd, now[2], now[3])
                now = ahead
            last(*held)
            dq3_s[place] = rope(dqt_s[...].T * 0.125, cos_s[...], sin_s[...], -1).astype(bf16)

        @pl.loop(0, 3)
        def _(c):
            @pl.loop(0, 2)
            def _(i):
                pair(2 * c + i, 6 * c + i)

                @pl.when(i == 0)
                def _():
                    red.tick(9 + 2 * c)
            for t in range(3):
                gwq = dot(h1t_s[...], joined(dq3_s, 6 * c + 2 * t, 2), 1, 0).astype(bf16)
                put_pieces(grad_s.at[c], gwq, 2 * t)
            red.tick(10 + 2 * c)

        @pl.loop(0, blocks)
        def _(i):
            blk = rows_of(i)
            dq3 = jnp.concatenate([dq3_s[n, blk, :] for n in range(18)], axis=1)
            dh = dot(dq3, joined(wq_s, 0, 18), 1, 1)
            unit, inverse = unit_rows(x_s[blk, :].astype(f32))
            gain_s[0, 0:1, :] += jnp.sum(dh * unit, axis=0, keepdims=True)
            scaled = dh * g1
            dmid_s[blk, :] += inverse * (scaled - unit * jnp.mean(scaled * unit, axis=-1, keepdims=True))
            dmb_s[blk, :] = mid_s[blk, :].astype(bf16)
        a = pltpu.make_async_copy(dmid_s, input_grad, store_sem.at[0])
        b = pltpu.make_async_copy(dmb_s, block_out, store_sem.at[1])
        a.start()
        b.start()
        step = 0
        pending = None
        while 15 + step <= red.last_tick() or step <= len(names):
            if pending is not None:
                pending.wait()
                gain_s[step] = gain_s[step - 1] + gain_s[len(names) + step]
                pending = None
            if step < len(names):
                pending = remote(gain_s.at[step], gain_s.at[len(names) + 1 + step], gsend_sem.at[step], grecv_sem.at[step],
                                 ids[names[step]])
                pending.start()
            red.tick(15 + step)
            step += 1
        gain_out[...] = pltpu.roll(gain_s[len(names)], width - fs * rows, 1)
        a.wait()
        b.wait()

    pairs = width // 128
    pl.run_scoped(attention, V((pairs, count, 128), bf16), V((pairs, count, 128), bf16), V((pairs, count, 128), bf16),
                  V((128, count), bf16), V((count, width), bf16), V((width, count), bf16), V((pairs, count, 128), bf16),
                  V((pairs, 8, count), f32),
                  V((count, width), bf16), V((18, count, 128), bf16), V((width, count), bf16), V((count, count), f32),
                  V((128, count), f32))
    for n in range(CHUNKS):
        red.store(n).wait()


def backward(reps, lengths, gain, tokens, cotangent, mid, q, k, v, a, at, h1t, log, cosine, sine, wq, wo, wf, wd):
    count, width = tokens.shape
    S = jax.ShapeDtypeStruct
    V = pltpu.VMEM
    dma = pltpu.SemaphoreType.DMA
    bits = reps.bit_length() - 1
    steps = 2 + bits
    exchanges = 10 + bits - 3
    lags = stage_lags(reps)
    shapes = [(2, 8), (8,), (4,), (3,)] + [(1,)] * (bits - 3)
    slots = [V((2 * lags[k],) + shape + (PIECE, 128), bf16) for k, shape in enumerate(shapes)]
    return pl.pallas_call(
        functools.partial(backward_kernel, reps),
        name="backward_reduce",
        in_specs=[SM, VM] + [ANY] * 16,
        out_specs=[ANY] * 3 + [VM],
        out_shape=[S((count, width), bf16), S((count, width), f32), S((CHUNKS, 8, PIECE, 128), bf16), S((8, width), f32)],
        scratch_shapes=[
            V((count, width), f32), V((count, width), f32), V((count, width), bf16), V((count, width), bf16),
            V((count, 128), f32), V((count, 128), f32), V((18, width, 128), bf16), V((6, width, 128), bf16),
            V((count, width), f32),
            V((SLOTS, 2, 2, 8, PIECE, 128), bf16), V((CHUNKS, 8, PIECE, 128), bf16), V((2 * steps + 1, 8, width), f32),
            dma((exchanges, 2 * max(lags))), dma((exchanges, 2 * max(lags))), dma((steps,)), dma((steps,)), dma((CHUNKS,)), dma((15,)), dma((2,))] + slots,
        compiler_params=pltpu.CompilerParams(collective_id=1, has_side_effects=True, vmem_limit_bytes=62 * 2**20),
    )(lengths, gain, tokens, cotangent, mid, q, k, v, a, at, h1t, log, cosine, sine, wq, wo, wf, wd)


def adamw(weight, first, second, grad, rate):
    first_new = beta_first * first + (1.0 - beta_first) * grad
    second_new = beta_second * second + (1.0 - beta_second) * grad * grad
    first_hat = first_new * (1.0 / (1.0 - beta_first**STEP))
    second_hat = second_new * (1.0 / (1.0 - beta_second**STEP))
    return (
        first_new,
        second_new,
        weight - rate * (first_hat / (jnp.sqrt(second_hat) + adam_eps) + decay_rate * weight),
    )


def update_tasks(width):
    rows = width // 4
    tasks = []
    for t in range(3):
        cols = [[(9 + c, r + 4 * ((2 * t + i) // 3), 48 * ((2 * t + i) % 3), 48) for r in range(4)]
                for c in range(3) for i in range(2)]
        tasks.append((0, (0, rows), t * width, cols))
    for k in range(8):
        tasks.append((2, (0, rows), 512 * k, [[(2 * j, k, 96, 48), (2 * j + 1, k, 0, 144)] for j in range(4)]))
    for j in range(4):
        tasks.append((3, (128 * j, 128), 0, [[(2 * j, k, 16 * c, 16) for k in range(8)] for c in range(6)]))
    tasks.append((1, (0, rows), 0, [[(8, r + 4 * (b // 3), 48 * (b % 3), 48) for r in range(4)] for b in range(6)]))
    return tasks


def update_kernel(rates, tasks, depth, grad_ref, gain_grad, *refs):
    state, refs = refs[:12], refs[12:]
    gain_state, refs = refs[:3], refs[3:]
    new, refs = refs[:12], refs[12:]
    gain_new, refs = refs[:3], refs[3:]
    taken, made, in_sem, out_sem = refs

    def moves(n, out):
        w, (row, rows), col, cols = tasks[n]
        wide = 128 * len(cols)
        slot = n % depth
        found = []
        for i in range(3):
            if out:
                found.append(pltpu.make_async_copy(made.at[slot, i, pl.ds(0, rows), pl.ds(0, wide)],
                                                   new[3 * w + i].at[pl.ds(row, rows), pl.ds(col, wide)], out_sem.at[slot, i]))
            else:
                found.append(pltpu.make_async_copy(state[3 * w + i].at[pl.ds(row, rows), pl.ds(col, wide)],
                                                   taken.at[slot, i, pl.ds(0, rows), pl.ds(0, wide)], in_sem.at[slot, i]))
        return found

    for n in range(depth):
        for c in moves(n, False):
            c.start()
    columns = gain_grad[0:2, 0:gain_new[0].shape[1]]
    for ref, value in zip((gain_new[1], gain_new[2], gain_new[0]), adamw(gain_state[0][...], gain_state[1][...], gain_state[2][...], columns, 1.0)):
        ref[...] = value
    for n, (w, (_, rows), _, cols) in enumerate(tasks):
        slot = n % depth
        for c in moves(n, False):
            c.wait()
        if n >= depth:
            for c in moves(n - depth, True):
                c.wait()
        for i, pieces in enumerate(cols):
            grad = jnp.concatenate([grad_ref[c, p, r:r + m, :] for c, p, r, m in pieces], axis=0).astype(f32)
            lanes = slice(128 * i, 128 * i + 128)
            held = [taken[slot, s, 0:rows, lanes] for s in range(3)]
            for s, value in zip((1, 2, 0), adamw(held[0], held[1], held[2], grad, rates[w])):
                made[slot, s, 0:rows, lanes] = value
        for c in moves(n, True):
            c.start()
        if n + depth < len(tasks):
            for c in moves(n + depth, False):
                c.start()
    for n in range(len(tasks) - depth, len(tasks)):
        for c in moves(n, True):
            c.wait()


def update(rates, grads, gain_grad, state, gain_state):
    width = gain_grad.shape[1]
    S = jax.ShapeDtypeStruct
    depth = 3
    dma = pltpu.SemaphoreType.DMA
    return pl.pallas_call(
        functools.partial(update_kernel, rates, update_tasks(width), depth),
        name="update",
        in_specs=[VM, VM] + [ANY] * 12 + [VM] * 3,
        out_specs=[ANY] * 12 + [VM] * 3,
        out_shape=[S(z.shape, f32) for z in state + gain_state],
        scratch_shapes=[pltpu.VMEM((depth, 3, width // 4, width), f32), pltpu.VMEM((depth, 3, width // 4, width), f32),
                        dma((depth, 3)), dma((depth, 3))],
        compiler_params=pltpu.CompilerParams(vmem_limit_bytes=60 * 2**20),
    )(grads, gain_grad, *state, *gain_state)


def shards(reps, tokens, cotangent, lengths, w_qkv, m_qkv, v_qkv, w_proj, m_proj, v_proj, w_ffn, m_ffn, v_ffn,
           w_down, m_down, v_down, gains, m_gains, v_gains):
    count, width = tokens.shape
    wq, wo, wf, wd, q, k, v, a, at, h1t, log, mid, gain, cosine, sine = forward(
        reps, lengths, tokens, gains, w_qkv, w_proj, w_ffn, w_down)
    block_out, input_grad, grads, gain_grad = backward(
        reps, lengths, gain, tokens, cotangent, mid, q, k, v, a, at, h1t, log, cosine, sine, wq, wo, wf, wd)
    wide = 3.0 * width ** (-0.5)
    proj = 3.0 * (count / (10.0 * width)) ** 0.5
    down = 6.0 * FF ** (-0.5)
    new = update(
        (wide, proj, wide, down), grads, gain_grad,
        (w_qkv, m_qkv, v_qkv, w_proj, m_proj, v_proj, w_ffn, m_ffn, v_ffn, w_down, m_down, v_down),
        (gains, m_gains, v_gains))
    return (block_out, input_grad) + tuple(new[3 * w + s] for w in range(5) for s in (1, 2, 0))


def solution(mesh):
    reps = mesh.shape["rep"]
    tokens = P(("rep", "fsdp"), None)
    weight = P("fsdp", None)
    gain = P(None, "fsdp")
    return jax.shard_map(
        functools.partial(shards, reps),
        mesh=mesh,
        in_specs=(tokens,) * 3 + (weight,) * 12 + (gain,) * 3,
        out_specs=(tokens,) * 2 + (weight,) * 12 + (gain,) * 3,
        check_vma=False,
    )
```

profile of v0, /device:TPU:0, one launch (start us, length us, event | category | flops | bytes accessed | tf_op | source)
XLA Modules:
  0.0 218.3 jit_solution(15194593594482374208)
XLA Ops:
  0.7 54.7 %gather_forward.1 = (bf16[18,768,128]{2,1,0:T(8,128)(2,1)}, bf16[6,768,128]{2,1,0:T(8,128)(2,1)}, bf16[32,768,128]{2,1,0:T(8,128)(2,1)}, bf16[4,512,768]{2,1,0:T...) custom-call(s32[1,4]{1,0:T(1,128)} %len_ref.3, ...), custom_call_target="tpu_custom_call" | custom-call | tf_op jit(solution)/shard_map/gather_forward/pallas_call | solution.py:404
  55.4 139.9 %backward_reduce.1 = (bf16[1024,768]{1,0:T(8,128)(2,1)}, f32[1024,768]{1,0:T(8,128)}, bf16[12,8,144,128]{3,2,1,0:T(8,128)(2,1)}, f32[8,768]{1,0:T(8,128)}) custom-call(s32[1,4]{1,0:T(1,128)} %len_ref.3, f32[8,768]{1,0:T(8,128)} %get-tuple-element.51.gain_ref, bf16[1024,768]{1,0:T(8,128)(2,1)} %x_in.3, bf16[1024,768]{1,0:T(8,128)(2,1)} %cot_in.1, ...), custom_call_target="tpu_custom_call" | custom-call | tf_op jit(solution)/shard_map/backward_reduce/pallas_call | solution.py:809
  195.3 0.0 copy-start.1
  195.3 18.9 %update.1 = (f32[192,2304]{1,0:T(8,128)}, f32[192,2304]{1,0:T(8,128)}, f32[192,2304]{1,0:T(8,128)}, f32[192,768]{1,0:T(8,128)}, f32[192,768]{1,0:T(8,128)}, /*in...) custom-call(bf16[12,8,144,128]{3,2,1,0:T(8,128)(2,1)} %get-tuple-ele, ...), custom_call_target="tpu_custom_call" | custom-call | tf_op jit(solution)/shard_map/update/pallas_call | solution.py:907
  214.2 0.0 copy-start
  214.2 0.0 copy-done.1
  214.2 1.1 copy.38
  215.3 1.3 copy-done
  216.6 1.7 copy.39
Async XLA Ops:
  195.3 18.9 %copy-start.1 = (bf16[1024,768]{1,0:T(8,128)(2,1)S(1)}, bf16[1024,768]{1,0:T(8,128)(2,1)}, u32[]{:S(2)}) copy-start(bf16[1024,768]{1,0:T(8,128)(2,1)} %get-tuple-element.102) | copy-start | bytes 4718596
  214.2 2.5 %copy-start = (f32[1024,768]{1,0:T(8,128)S(1)}, f32[1024,768]{1,0:T(8,128)}, u32[]{:S(2)}) copy-start(f32[1024,768]{1,0:T(8,128)} %get-tuple-element.103) | copy-start | bytes 9437188
where the time goes:
time: 219 us; the launch traced here: 218 us
  Pallas kernels  213 us (97%)
  local copies, waits for them, and re-layouts  4.11 us (2%)
    pallas_call x1, Pallas kernels, backward(): pl.pallas_call(functools.partial(backward_kernel, reps), name='backward_r...  140 us
    pallas_call x1, Pallas kernels, forward(): pl.pallas_call(functools.partial(forward_kernel, reps), name='gather_forw...  54.7 us
    pallas_call x1, Pallas kernels, update(): pl.pallas_call(functools.partial(update_kernel, rates, update_tasks(width...  18.9 us

commit v1 on v0

--- a/solution.py
+++ b/solution.py
@@ -26,7 +26,7 @@
 CHUNKS = 12
 PIECE = 144
 SLOTS = 9
-LAGS = (2, 2, 2, 2, 2)
+LAGS = (2, 2, 3, 3, 3)
 ANY = pl.BlockSpec(memory_space=pl.ANY)
 VM = pl.BlockSpec(memory_space=pltpu.VMEM)
 SM = pl.BlockSpec(memory_space=pltpu.SMEM)
@@ -270,9 +270,7 @@
         blk = pl.ds(pl.multiple_of(i * BLK, BLK), BLK)
         x = x_s[blk, :].astype(f32)
         inverse = lax.rsqrt(jnp.mean(x * x, axis=-1, keepdims=True) + norm_eps)
-        h1 = x * inverse * g1
-        h1_s[blk, :] = h1.astype(bf16)
-        h1t_s[:, blk] = h1.T.astype(bf16)
+        h1_s[blk, :] = (x * inverse * g1).astype(bf16)
 
     near[0].second()
     wide[0].second()
@@ -332,7 +330,7 @@
             a_s[i * BLK:(i + 1) * BLK, cols] = both.T.astype(bf16)
 
     ready = [pltpu.make_async_copy(src, dst, store_sem.at[3 + i]) for i, (src, dst) in enumerate((
-        (wq_s, wq_out), (q_s, q_out), (k_s, k_out), (v_s, v_out), (cos_s, cos_out), (sin_s, sin_out), (h1t_s, h1t_out)))]
+        (wq_s, wq_out), (q_s, q_out), (k_s, k_out), (v_s, v_out), (cos_s, cos_out), (sin_s, sin_out)))]
     arrivals = [[near[0].arrive], [near[1].arrive], [near[2].arrive]]
     projected = [
         [near[2].fourth, wide[1].second, wide[0].third, down.start],
@@ -378,6 +376,14 @@
         blk = pl.ds(pl.multiple_of(i * BLK, BLK), BLK)
         mid_s[blk, :] = x_s[blk, :].astype(f32) + dot(a_s[blk, :], joined(wo_s, 0, 6), 1, 0)
     c = pltpu.make_async_copy(mid_s, mid_out, store_sem.at[14])
+    c.start()
+    stores.append(c)
+
+    @pl.loop(0, count // BLK)
+    def _(i):
+        blk = pl.ds(pl.multiple_of(i * BLK, BLK), BLK)
+        h1t_s[:, blk] = h1_s[blk, :].astype(f32).T.astype(bf16)
+    c = pltpu.make_async_copy(h1t_s, h1t_out, store_sem.at[9])
     c.start()
     stores.append(c)
     for g in wide + [down]:
@@ -764,13 +770,16 @@
             scaled = dh * g1
             dmid_s[blk, :] += inverse * (scaled - unit * jnp.mean(scaled * unit, axis=-1, keepdims=True))
             dmb_s[blk, :] = mid_s[blk, :].astype(bf16)
+            red.tick(15 + i)
+
         a = pltpu.make_async_copy(dmid_s, input_grad, store_sem.at[0])
         b = pltpu.make_async_copy(dmb_s, block_out, store_sem.at[1])
         a.start()
         b.start()
         step = 0
         pending = None
-        while 15 + step <= red.last_tick() or step <= len(names):
+        drain = 15 + blocks
+        while drain + step <= red.last_tick() or step <= len(names):
             if pending is not None:
                 pending.wait()
                 gain_s[step] = gain_s[step - 1] + gain_s[len(names) + step]
@@ -779,7 +788,7 @@
                 pending = remote(gain_s.at[step], gain_s.at[len(names) + 1 + step], gsend_sem.at[step], grecv_sem.at[step],
                                  ids[names[step]])
                 pending.start()
-            red.tick(15 + step)
+            red.tick(drain + step)
             step += 1
         gain_out[...] = pltpu.roll(gain_s[len(names)], width - fs * rows, 1)
         a.wait()
@@ -850,11 +859,16 @@
 
 
 def update_kernel(rates, tasks, depth, grad_ref, gain_grad, *refs):
+    passed, refs = refs[:2], refs[2:]
     state, refs = refs[:12], refs[12:]
     gain_state, refs = refs[:3], refs[3:]
     new, refs = refs[:12], refs[12:]
     gain_new, refs = refs[:3], refs[3:]
-    taken, made, in_sem, out_sem = refs
+    given, refs = refs[:2], refs[2:]
+    taken, made, in_sem, out_sem, low_s, wide_s, pass_sem = refs
+    holds = (low_s, wide_s)
+    through = [pltpu.make_async_copy(passed[i], holds[i], pass_sem.at[i]) for i in range(2)]
+    onward = [pltpu.make_async_copy(holds[i], given[i], pass_sem.at[2 + i]) for i in range(2)]
 
     def moves(n, out):
         w, (row, rows), col, cols = tasks[n]
@@ -894,26 +908,36 @@
         if n + depth < len(tasks):
             for c in moves(n + depth, False):
                 c.start()
+        if n == 2:
+            for c in through:
+                c.start()
+        if n == 8:
+            for a, b in zip(through, onward):
+                a.wait()
+                b.start()
     for n in range(len(tasks) - depth, len(tasks)):
         for c in moves(n, True):
             c.wait()
-
-
-def update(rates, grads, gain_grad, state, gain_state):
+    for c in onward:
+        c.wait()
+
+
+def update(rates, grads, gain_grad, through, state, gain_state):
     width = gain_grad.shape[1]
     S = jax.ShapeDtypeStruct
-    depth = 3
+    depth = 6
     dma = pltpu.SemaphoreType.DMA
     return pl.pallas_call(
         functools.partial(update_kernel, rates, update_tasks(width), depth),
         name="update",
-        in_specs=[VM, VM] + [ANY] * 12 + [VM] * 3,
-        out_specs=[ANY] * 12 + [VM] * 3,
-        out_shape=[S(z.shape, f32) for z in state + gain_state],
+        in_specs=[VM, VM] + [ANY] * 14 + [VM] * 3,
+        out_specs=[ANY] * 12 + [VM] * 3 + [ANY] * 2,
+        out_shape=[S(z.shape, z.dtype) for z in state + gain_state + through],
         scratch_shapes=[pltpu.VMEM((depth, 3, width // 4, width), f32), pltpu.VMEM((depth, 3, width // 4, width), f32),
-                        dma((depth, 3)), dma((depth, 3))],
+                        dma((depth, 3)), dma((depth, 3))]
+        + [pltpu.VMEM(z.shape, z.dtype) for z in through] + [dma((4,))],
         compiler_params=pltpu.CompilerParams(vmem_limit_bytes=60 * 2**20),
-    )(grads, gain_grad, *state, *gain_state)
+    )(grads, gain_grad, *through, *state, *gain_state)
 
 
 def shards(reps, tokens, cotangent, lengths, w_qkv, m_qkv, v_qkv, w_proj, m_proj, v_proj, w_ffn, m_ffn, v_ffn,
@@ -927,10 +951,10 @@
     proj = 3.0 * (count / (10.0 * width)) ** 0.5
     down = 6.0 * FF ** (-0.5)
     new = update(
-        (wide, proj, wide, down), grads, gain_grad,
+        (wide, proj, wide, down), grads, gain_grad, (block_out, input_grad),
         (w_qkv, m_qkv, v_qkv, w_proj, m_proj, v_proj, w_ffn, m_ffn, v_ffn, w_down, m_down, v_down),
         (gains, m_gains, v_gains))
-    return (block_out, input_grad) + tuple(new[3 * w + s] for w in range(5) for s in (1, 2, 0))
+    return (new[15], new[16]) + tuple(new[3 * w + s] for w in range(5) for s in (1, 2, 0))
 
 
 def solution(mesh):

time: 219 us -> 216 us (0.986)
  local copies, waits for them, and re-layouts: 4.11 us -> 0 us
    unnamed x6 -> x0, local copies, waits for them, and re-layouts: 4.11 us -> none
    pallas_call x1, Pallas kernels: 18.9 us -> 21.5 us  [update(): pl.pallas_call(functools.partial(update_kernel, rates, update_tasks(width...]
where the time goes in v1:
time: 216 us
  Pallas kernels  215 us (100%)
    pallas_call x1, Pallas kernels, backward(): pl.pallas_call(functools.partial(backward_kernel, reps), name='backward_r...  138 us
    pallas_call x1, Pallas kernels, forward(): pl.pallas_call(functools.partial(forward_kernel, reps), name='gather_forw...  55.3 us
    pallas_call x1, Pallas kernels, update(): pl.pallas_call(functools.partial(update_kernel, rates, update_tasks(width...  21.5 us

profile of v1, /device:TPU:0, one launch (start us, length us, event | category | flops | bytes accessed | tf_op | source)
XLA Modules:
  0.0 215.5 jit_solution(302314753705993389)
XLA Ops:
  0.7 55.3 %gather_forward.1 = (bf16[18,768,128]{2,1,0:T(8,128)(2,1)}, bf16[6,768,128]{2,1,0:T(8,128)(2,1)}, bf16[32,768,128]{2,1,0:T(8,128)(2,1)}, bf16[4,512,768]{2,1,0:T...) custom-call(s32[1,4]{1,0:T(1,128)} %len_ref.3, ...), custom_call_target="tpu_custom_call" | custom-call | tf_op jit(solution)/shard_map/gather_forward/pallas_call | solution.py:410
  55.9 137.9 %backward_reduce.1 = (bf16[1024,768]{1,0:T(8,128)(2,1)}, f32[1024,768]{1,0:T(8,128)}, bf16[12,8,144,128]{3,2,1,0:T(8,128)(2,1)}, f32[8,768]{1,0:T(8,128)}) custom-call(s32[1,4]{1,0:T(1,128)} %len_ref.3, f32[8,768]{1,0:T(8,128)} %get-tuple-element.53.gain_ref, bf16[1024,768]{1,0:T(8,128)(2,1)} %x_in.3, bf16[1024,768]{1,0:T(8,128)(2,1)} %cot_in.1, ...), custom_call_target="tpu_custom_call" | custom-call | tf_op jit(solution)/shard_map/backward_reduce/pallas_call | solution.py:818
  193.9 21.5 %update.1 = (f32[192,2304]{1,0:T(8,128)}, f32[192,2304]{1,0:T(8,128)}, f32[192,2304]{1,0:T(8,128)}, f32[192,768]{1,0:T(8,128)}, f32[192,768]{1,0:T(8,128)}, /*in...) custom-call(bf16[12,8,144,128]{3,2,1,0:T(8,128)(2,1)} %get-tuple-ele, ...), custom_call_target="tpu_custom_call" | custom-call | tf_op jit(solution)/shard_map/update/pallas_call | solution.py:930

commit v2 on v1

--- a/solution.py
+++ b/solution.py
@@ -173,11 +173,13 @@
     return found
 
 
-def meet(ids, names):
-    barrier = pltpu.get_barrier_semaphore()
+def greet(ids, names):
     for name in names:
-        pl.semaphore_signal(barrier, inc=1, device_id=ids[name], device_id_type=MESH)
-    pl.semaphore_wait(barrier, len(names))
+        pl.semaphore_signal(pltpu.get_barrier_semaphore(), inc=1, device_id=ids[name], device_id_type=MESH)
+
+
+def meet(names):
+    pl.semaphore_wait(pltpu.get_barrier_semaphore(), len(names))
 
 
 def place_gains(ref, rows, fs):
@@ -204,7 +206,9 @@
     gain_a[...] = jnp.zeros_like(gain_a)
     gain_a[0:2, 0:rows] = gain_in[...].astype(bf16).astype(f32)
     gain_a[...] = pltpu.roll(gain_a[...], fs * rows, 1)
-    meet(ids, ("core", "y", "bit0", "bit1"))
+    friends = ("core", "y", "bit0", "bit1")
+    greet(ids, friends)
+    meet(friends)
 
     sems = (send_sem, recv_sem)
     near = [Gather(None, wq_s, 6 * c, 6, rows, sems, c, ids, c == 0) for c in range(3)]
@@ -586,6 +590,7 @@
     g1, g2 = gain_ref[0:1, :], gain_ref[1:2, :]
 
     def feed(wf_s, wd_s, h2_s, h2t_s, z_s, df_s):
+        greet(ids, friends)
         need = [load(0, mid_in, mid_s), load(1, cot_in, dy_s)]
         def weights(j):
             return [pltpu.make_async_copy(wf_in.at[pl.ds(8 * j, 8)], wf_s.at[pl.ds(8 * j, 8)], load_sem.at[2 + 2 * j]),
@@ -596,7 +601,6 @@
                 c.start()
         late = [load(10, x_in, x_s), load(11, cos_in, cos_s), load(12, sin_in, sin_s), load(13, wq_in, wq_s),
                 load(14, wo_in, wo_s)]
-        meet(ids, friends)
         for c in need:
             c.wait()
 
@@ -611,6 +615,8 @@
             dy_s[blk, :] = jnp.where(token < valid, dy_s[blk, :], 0)
             out_s[blk, :] = mid_s[blk, :]
             dmid_s[blk, :] = jnp.zeros((BLK, width), f32)
+
+        meet(friends)
 
         @pl.loop(0, 4)
         def _(j):
@@ -676,8 +682,6 @@
             dmb_s[blk, :] = dmid.astype(bf16)
             mid_s[blk, :] = out_s[blk, :]
         red.tick(7)
-        for c in need:
-            c.wait()
 
         @pl.loop(0, 3)
         def _(c):
@@ -686,11 +690,14 @@
             da = dot(dmb_s[...], weight, 1, 1).astype(bf16)
             da_s[2 * c] = da[:, 0:128]
             da_s[2 * c + 1] = da[:, 128:256]
+        need[5].wait()
         for n in range(3):
             gwo = dot(at_s[...], dmb_s[:, 256 * n:256 * n + 256], 1, 0).astype(bf16)
             put_pieces(grad_s.at[8], gwo, 2 * n)
         red.tick(8)
         fill_bias(ends, bias, count)
+        for c in need[:5] + need[6:]:
+            c.wait()
 
         def pair(p, place):
             kt_s[...] = k_s[p].T

time: 216 us -> 216 us (level)
  no operation moved by 1% of the time
where the time goes in v2:
time: 216 us
  Pallas kernels  215 us (100%)
    pallas_call x1, Pallas kernels, backward(): pl.pallas_call(functools.partial(backward_kernel, reps), name='backward_r...  138 us
    pallas_call x1, Pallas kernels, forward(): pl.pallas_call(functools.partial(forward_kernel, reps), name='gather_forw...  55.3 us
    pallas_call x1, Pallas kernels, update(): pl.pallas_call(functools.partial(update_kernel, rates, update_tasks(width...  21.5 us

profile of v2, /device:TPU:0, one launch (start us, length us, event | category | flops | bytes accessed | tf_op | source)
XLA Modules:
  0.0 215.6 jit_solution(4079907167611795302)
XLA Ops:
  0.7 55.3 %gather_forward.1 = (bf16[18,768,128]{2,1,0:T(8,128)(2,1)}, bf16[6,768,128]{2,1,0:T(8,128)(2,1)}, bf16[32,768,128]{2,1,0:T(8,128)(2,1)}, bf16[4,512,768]{2,1,0:T...) custom-call(s32[1,4]{1,0:T(1,128)} %len_ref.3, ...), custom_call_target="tpu_custom_call" | custom-call | tf_op jit(solution)/shard_map/gather_forward/pallas_call | solution.py:414
  55.9 138.0 %backward_reduce.1 = (bf16[1024,768]{1,0:T(8,128)(2,1)}, f32[1024,768]{1,0:T(8,128)}, bf16[12,8,144,128]{3,2,1,0:T(8,128)(2,1)}, f32[8,768]{1,0:T(8,128)}) custom-call(s32[1,4]{1,0:T(1,128)} %len_ref.3, f32[8,768]{1,0:T(8,128)} %get-tuple-element.53.gain_ref, bf16[1024,768]{1,0:T(8,128)(2,1)} %x_in.3, bf16[1024,768]{1,0:T(8,128)(2,1)} %cot_in.1, ...), custom_call_target="tpu_custom_call" | custom-call | tf_op jit(solution)/shard_map/backward_reduce/pallas_call | solution.py:825
  193.9 21.5 %update.1 = (f32[192,2304]{1,0:T(8,128)}, f32[192,2304]{1,0:T(8,128)}, f32[192,2304]{1,0:T(8,128)}, f32[192,768]{1,0:T(8,128)}, f32[192,768]{1,0:T(8,128)}, /*in...) custom-call(bf16[12,8,144,128]{3,2,1,0:T(8,128)(2,1)} %get-tuple-ele, ...), custom_call_target="tpu_custom_call" | custom-call | tf_op jit(solution)/shard_map/update/pallas_call | solution.py:937
